TPU v7x, 32 devices: a whole 2x2x4 slice. The times are simulated.
32 devices in a mesh: rad: 4 (over x, core), sec: 8 (over z, y).
Axes of the slice: x: 2, y: 2, z: 4, core: 2. Of those that a mesh axis runs over, the one named last changes fastest.
Arguments:
- gas_fields: float32 [5, 128, 16, 2048], P(None, 'rad', None, 'sec'), may hold values from -8 to 8, as said below
- orbit_shift: int32 [128], P('rad'), may hold values from 0 to 2047
- particle_velocity: float32 [3, 131072], P(None, ('rad', 'sec')), may hold values from -6 to 6
- particle_mass: float32 [131072], P(('rad', 'sec')), may hold values from 0.2 to 2
- particle_stop: float32 [131072], P(('rad', 'sec')), may hold values from 0.1 to 10
- particle_cell: int32 [131072], P(('rad', 'sec')), may hold values from 0 to 131071
- particle_dest: int32 [131072, 1], P(('rad', 'sec')), may hold values from 0 to 31; in each aligned block of 4096 rows (0 to 4095, 4096 to 8191, ...) at most 256 rows name the same one
Outputs:
- gas_next: float32 [5, 128, 16, 2048], P(None, 'rad', None, 'sec')
- arrived_velocity: float32 [3, 262144], P(None, ('rad', 'sec'))
Inputs may be any that keep to these rules, and one draw needn't show every extreme that they name: `gas_fields`: field 0 (density) lies between 0.25 and 4 and momentum over density between -2 and 2. `particle_dest`: among the 4096 particles of one device at most 256 name the same destination; in every draw some device sends exactly 256 to one destination.
All inputs are finite; a program needn't handle non-finite values.
Results may differ from a plain program's by a relative error of at most 0.0003.
Values sent between devices are 32-bit elements; how exact they have to be, the bound alone decides.
A program may use at most 128 MiB of HBM per device.

v0:
```python
import jax
import jax.numpy as jnp
from jax import lax
from jax.sharding import PartitionSpec as P

sound_speed = 1.0
radial_rate = 0.2
azimuth_rate = 0.2
exact = lax.Precision.HIGHEST


def passed_along(block, axis, distance):
    devices = range(lax.axis_size(axis))
    route = [((i - distance) % len(devices), i) for i in devices]
    return lax.ppermute(block, axis, route)


def with_halo(cells, sides, width, closed):
    for axis, dim in sides:
        count = lax.axis_size(axis)
        ends = count if closed else count - 1
        head = lax.slice_in_dim(cells, 0, width, axis=dim)
        tail = lax.slice_in_dim(cells, cells.shape[dim] - width, cells.shape[dim], axis=dim)
        cells = jnp.concatenate(
            [
                lax.ppermute(tail, axis, [(i, (i + 1) % count) for i in range(ends)]),
                cells,
                lax.ppermute(head, axis, [((i + 1) % count, i) for i in range(ends)]),
            ],
            axis=dim,
        )
    return cells


def limited_slope(left_step, right_step):
    return (
        0.5
        * (jnp.sign(left_step) + jnp.sign(right_step))
        * jnp.minimum(jnp.abs(left_step), jnp.abs(right_step))
    )


def plm_divergence(values, speed, along_axis, extent):

    def take_range(source, offset_at, length):
        return lax.slice_in_dim(source, offset_at, offset_at + length, axis=along_axis)

    left_step = take_range(values, 1, extent + 2) - take_range(values, 0, extent + 2)
    right_step = take_range(values, 2, extent + 2) - take_range(values, 1, extent + 2)
    slopes = limited_slope(left_step, right_step)
    centre = take_range(values, 1, extent + 2)
    left_value = take_range(centre, 0, extent + 1) + 0.5 * take_range(slopes, 0, extent + 1)
    right_value = take_range(centre, 1, extent + 1) - 0.5 * take_range(slopes, 1, extent + 1)
    face_speed = 0.5 * (take_range(speed, 1, extent + 1) + take_range(speed, 2, extent + 1))
    face_flux = face_speed * 0.5 * (left_value + right_value) - 0.5 * (
        jnp.abs(face_speed) + sound_speed
    ) * (right_value - left_value)
    return take_range(face_flux, 1, extent) - take_range(face_flux, 0, extent)


def local(
    gas_fields,
    orbit_shift,
    particle_velocity,
    particle_mass,
    particle_stop,
    particle_cell,
    particle_dest,
):
    field_count, radius_count, layers, sector = gas_fields.shape
    sectors = lax.axis_size("sec")
    quotient = orbit_shift // sector
    remainder = orbit_shift % sector
    carried = gas_fields
    for bit_level in range(sectors.bit_length() - 1):
        incoming = passed_along(carried, "sec", 1 << bit_level)
        chosen = quotient >> bit_level & 1 == 1
        carried = jnp.where(chosen[None, :, None, None], incoming, carried)
    preceding = passed_along(carried, "sec", 1)
    window = jnp.concatenate([preceding, carried], axis=3)
    for bit_level in range((sector - 1).bit_length()):
        step_size = 1 << bit_level
        moved = jnp.concatenate(
            [
                jnp.zeros((field_count, radius_count, layers, step_size), jnp.float32),
                window[..., :-step_size],
            ],
            axis=3,
        )
        chosen = remainder >> bit_level & 1 == 1
        window = jnp.where(chosen[None, :, None, None], moved, window)
    shifted = window[..., sector:]
    per_device = particle_dest.shape[0]
    devices = lax.axis_size(("rad", "sec"))
    capacity = 2 * per_device // devices
    target = particle_dest[:, 0]
    hits = target[:, None] == jnp.arange(devices, dtype=jnp.int32)[None, :]
    order_index = jnp.arange(per_device, dtype=jnp.int32)
    earlier = (order_index[:, None] >= order_index[None, :]).astype(jnp.bfloat16)
    running = jnp.dot(earlier, hits.astype(jnp.bfloat16), preferred_element_type=jnp.float32)
    slot = jnp.sum(jnp.where(hits, running, 0.0), axis=1).astype(jnp.int32) - 1
    column = target * capacity + slot
    records = jnp.concatenate(
        [
            particle_velocity,
            particle_mass[None],
            particle_stop[None],
            particle_cell[None].astype(jnp.float32),
        ],
        axis=0,
    )
    block_rows = min(512, per_device)
    block_count = per_device // block_rows
    record_blocks = records.reshape(6, block_count, block_rows).transpose(1, 0, 2)
    column_blocks = column.reshape(block_count, block_rows)
    slot_ids = jnp.arange(devices * capacity, dtype=jnp.int32)

    def place_block(total, pair):
        record_block, column_block = pair
        placing = (column_block[:, None] == slot_ids[None, :]).astype(jnp.float32)
        return (
            total
            + jnp.dot(record_block, placing, precision=exact, preferred_element_type=jnp.float32),
            None,
        )

    outbox_flat, _ = lax.scan(
        place_block, jnp.zeros((6, devices * capacity), jnp.float32), (record_blocks, column_blocks)
    )
    outbox = outbox_flat.reshape(6, devices, capacity)
    inbox = lax.all_to_all(outbox, ("rad", "sec"), split_axis=1, concat_axis=1, tiled=True)
    received = inbox.reshape(6, devices * capacity)
    row_count = radius_count * layers
    velocity_rows = (
        (shifted[1:4] / shifted[0:1])
        .reshape(3, row_count, sector)
        .transpose(1, 0, 2)
        .reshape(row_count, 3 * sector)
    )
    cells = received[5].astype(jnp.int32)
    row_hot = (
        (cells // sector)[:, None] == jnp.arange(row_count, dtype=jnp.int32)[None, :]
    ).astype(jnp.float32)
    azimuth_hot = (
        (cells % sector)[:, None] == jnp.arange(sector, dtype=jnp.int32)[None, :]
    ).astype(jnp.float32)
    picked = jnp.dot(
        row_hot, velocity_rows, precision=exact, preferred_element_type=jnp.float32
    ).reshape(-1, 3, sector)
    local_speed = jnp.sum(picked * azimuth_hot[:, None, :], axis=2).T
    velocity_in = received[0:3]
    fraction = received[4] / (1.0 + received[4])
    change = (velocity_in - local_speed) * fraction[None]
    arrived_velocity = velocity_in - change
    impulse = received[3][None] * change
    spread = (impulse.T[:, :, None] * azimuth_hot[:, None, :]).reshape(-1, 3 * sector)
    deposit_rows = jnp.dot(row_hot.T, spread, precision=exact, preferred_element_type=jnp.float32)
    momentum_added = (
        deposit_rows.reshape(row_count, 3, sector)
        .transpose(1, 0, 2)
        .reshape(3, radius_count, layers, sector)
    )
    dragged = jnp.concatenate([shifted[0:1], shifted[1:4] + momentum_added, shifted[4:5]], axis=0)
    radial_speed = dragged[1] / dragged[0]
    azimuthal_speed = dragged[2] / dragged[0]
    stacked = jnp.concatenate([dragged, radial_speed[None], azimuthal_speed[None]], axis=0)
    radial_pad = with_halo(stacked, (("rad", 1),), 2, False)
    azimuth_pad = with_halo(stacked, (("sec", 3),), 2, True)
    radial_change = plm_divergence(radial_pad[0:5], radial_pad[5:6], 1, radius_count)
    azimuth_change = plm_divergence(azimuth_pad[0:5], azimuth_pad[6:7], 3, sector)
    gas_next = dragged - radial_rate * radial_change - azimuth_rate * azimuth_change
    return (gas_next, arrived_velocity)


def solution(mesh):
    placed = (
        P(None, "rad", None, "sec"),
        P("rad"),
        P(None, ("rad", "sec")),
        P(("rad", "sec")),
        P(("rad", "sec")),
        P(("rad", "sec")),
        P(("rad", "sec"), None),
    )
    return jax.shard_map(
        local,
        mesh=mesh,
        in_specs=placed,
        out_specs=(P(None, "rad", None, "sec"), P(None, ("rad", "sec"))),
        check_vma=False,
    )
```

profile of v0, /device:TPU:0, one launch (start us, length us, event | category | flops | bytes accessed | tf_op | source)
XLA Modules:
  0.0 425.9 jit_solution(14129151477188289816)
XLA Ops:
  0.6 3.0 collective-permute-start
  4.3 59.4 %collective-permute-done = f32[5,32,16,256]{3,2,1,0:T(8,128)S(1)} collective-permute-done((f32[5,32,16,256]{3,2,1,0:T(8,128)}, f32[5,32,16,256]{3,2,1,0:T(8,128)S(1)}, u32[]{:S(2)}, u32[]{:S(2)}) %collective-permute-start) | collective-permute-done | bytes 2621472 | tf_op jit(solution)/shard_map/ppermute | solution.py:15
  63.8 2.1 broadcast_select_fusion
  66.1 17.1 %fusion.41 = f32[4096]{0:T(1024)S(1)} fusion(s32[4096]{0:T(1024)S(1)} %bitcast.90), kind=kOutput, calls=%fused_computation.85 | convolution fusion | flops 1091039232 | bytes 32768 | tf_op jit(solution)/shard_map/dot_general | solution.py:100
  83.4 42.6 %collective-permute-done.1 = f32[5,32,16,256]{3,2,1,0:T(8,128)} collective-permute-done((f32[5,32,16,256]{3,2,1,0:T(8,128)S(1)}, f32[5,32,16,256]{3,2,1,0:T(8,128)}, u32[]{:S(2)}, u32[]{:S(2)}) %collective-permute-start.1) | collective-permute-done | bytes 2621472 | tf_op jit(solution)/shard_map/ppermute | solution.py:15
  125.9 2.8 broadcast_select_fusion.1
  128.9 55.6 %while.11 = (s32[]{:T(128)}, f32[6,8192]{1,0:T(8,128)}, f32[8,6,512]{2,1,0:T(8,128)S(1)}, s32[8,512]{1,0:T(8,128)S(1)}, s32[]{:T(128)}, /*index=5*/s32[]{:T(128)}) while((s32[]{:T(128)}, f32[6,8192]{1,0:T(8,128)}, f32[8,6,512]{2,1,0:T(8,128)S(1)}, s32[8,512]{1,0:T(8,128)S(1)}, s32[]{:T(128)}, /*index=5*/s32[]{:T(128)}) %tuple.49), condition=%wide.region_2.3_spmd.clone, body=%wide.region_1.2_spmd.clone.sunk | while | flops 306282496 | bytes 415839 | solution.py:127
  128.9 6.1 %fusion.60 = f32[6,8192]{1,0:T(8,128)} fusion(s32[512]{0:T(512)S(1)} %bitcast.89, f32[6,8192]{1,0:T(8,128)} %get-tuple-element.123, pred[]{:T(512)S(6)} %compare.25, f32[8,6,512]{2,1,0:T(8,128)S(1)} %get-tuple-element.130, s32[]{:T(128)S(6)} %copy.26), kind=kOutput, calls=%fused_computation.3.clone.1 | convolution fusion | flops 306282496 | bytes 411653 | tf_op jit(solution)/shard_map/while/body/eval_jaxpr/dot_general | solution.py:123
  135.0 7.1 %fusion.60 = f32[6,8192]{1,0:T(8,128)} fusion(s32[512]{0:T(512)S(1)} %bitcast.89, f32[6,8192]{1,0:T(8,128)} %get-tuple-element.123, pred[]{:T(512)S(6)} %compare.25, f32[8,6,512]{2,1,0:T(8,128)S(1)} %get-tuple-element.130, s32[]{:T(128)S(6)} %copy.26), kind=kOutput, calls=%fused_computation.3.clone.1 | convolution fusion | flops 306282496 | bytes 411653 | tf_op jit(solution)/shard_map/while/body/eval_jaxpr/dot_general | solution.py:123
  142.1 7.1 %fusion.60 = f32[6,8192]{1,0:T(8,128)} fusion(s32[512]{0:T(512)S(1)} %bitcast.89, f32[6,8192]{1,0:T(8,128)} %get-tuple-element.123, pred[]{:T(512)S(6)} %compare.25, f32[8,6,512]{2,1,0:T(8,128)S(1)} %get-tuple-element.130, s32[]{:T(128)S(6)} %copy.26), kind=kOutput, calls=%fused_computation.3.clone.1 | convolution fusion | flops 306282496 | bytes 411653 | tf_op jit(solution)/shard_map/while/body/eval_jaxpr/dot_general | solution.py:123
  149.2 7.1 %fusion.60 = f32[6,8192]{1,0:T(8,128)} fusion(s32[512]{0:T(512)S(1)} %bitcast.89, f32[6,8192]{1,0:T(8,128)} %get-tuple-element.123, pred[]{:T(512)S(6)} %compare.25, f32[8,6,512]{2,1,0:T(8,128)S(1)} %get-tuple-element.130, s32[]{:T(128)S(6)} %copy.26), kind=kOutput, calls=%fused_computation.3.clone.1 | convolution fusion | flops 306282496 | bytes 411653 | tf_op jit(solution)/shard_map/while/body/eval_jaxpr/dot_general | solution.py:123
  156.2 7.1 %fusion.60 = f32[6,8192]{1,0:T(8,128)} fusion(s32[512]{0:T(512)S(1)} %bitcast.89, f32[6,8192]{1,0:T(8,128)} %get-tuple-element.123, pred[]{:T(512)S(6)} %compare.25, f32[8,6,512]{2,1,0:T(8,128)S(1)} %get-tuple-element.130, s32[]{:T(128)S(6)} %copy.26), kind=kOutput, calls=%fused_computation.3.clone.1 | convolution fusion | flops 306282496 | bytes 411653 | tf_op jit(solution)/shard_map/while/body/eval_jaxpr/dot_general | solution.py:123
  163.3 7.1 %fusion.60 = f32[6,8192]{1,0:T(8,128)} fusion(s32[512]{0:T(512)S(1)} %bitcast.89, f32[6,8192]{1,0:T(8,128)} %get-tuple-element.123, pred[]{:T(512)S(6)} %compare.25, f32[8,6,512]{2,1,0:T(8,128)S(1)} %get-tuple-element.130, s32[]{:T(128)S(6)} %copy.26), kind=kOutput, calls=%fused_computation.3.clone.1 | convolution fusion | flops 306282496 | bytes 411653 | tf_op jit(solution)/shard_map/while/body/eval_jaxpr/dot_general | solution.py:123
  170.4 7.1 %fusion.60 = f32[6,8192]{1,0:T(8,128)} fusion(s32[512]{0:T(512)S(1)} %bitcast.89, f32[6,8192]{1,0:T(8,128)} %get-tuple-element.123, pred[]{:T(512)S(6)} %compare.25, f32[8,6,512]{2,1,0:T(8,128)S(1)} %get-tuple-element.130, s32[]{:T(128)S(6)} %copy.26), kind=kOutput, calls=%fused_computation.3.clone.1 | convolution fusion | flops 306282496 | bytes 411653 | tf_op jit(solution)/shard_map/while/body/eval_jaxpr/dot_general | solution.py:123
  177.4 7.1 %fusion.60 = f32[6,8192]{1,0:T(8,128)} fusion(s32[512]{0:T(512)S(1)} %bitcast.89, f32[6,8192]{1,0:T(8,128)} %get-tuple-element.123, pred[]{:T(512)S(6)} %compare.25, f32[8,6,512]{2,1,0:T(8,128)S(1)} %get-tuple-element.130, s32[]{:T(128)S(6)} %copy.26), kind=kOutput, calls=%fused_computation.3.clone.1 | convolution fusion | flops 306282496 | bytes 411653 | tf_op jit(solution)/shard_map/while/body/eval_jaxpr/dot_general | solution.py:123
  184.5 4.0 all-to-all-start
  188.5 57.8 %all-to-all-done = f32[6,32,256]{2,0,1:T(8,128)S(1)} async-done(((f32[6,32,256]{2,0,1:T(8,128)}), f32[6,32,256]{2,0,1:T(8,128)S(1)}, u32[]{:S(2)}, u32[]{:S(2)}) %all-to-all-start) | async-done | bytes 196640 | tf_op jit(solution)/shard_map/all_to_all | solution.py:131
  246.3 2.2 broadcast_select_fusion.2
  248.4 3.1 collective-permute-start.3
  251.7 4.3 %fusion.20 = f32[8192,256]{0,1:T(8,128)} fusion(s32[8192]{0:T(1024)S(1)} %get-tuple-element.79), kind=kLoop, calls=%fused_computation.23 | loop fusion | flops 4194304 | bytes 8421376 | tf_op jit(solution)/shard_map/convert_element_type | solution.py:146
  256.0 54.6 %collective-permute-done.3 = f32[5,32,16,256]{3,2,1,0:T(8,128)S(1)} collective-permute-done((f32[5,32,16,256]{3,2,1,0:T(8,128)S(1)}, f32[5,32,16,256]{3,2,1,0:T(8,128)S(1)}, u32[]{:S(2)}, u32[]{:S(2)}) %collective-permute-start.3) | collective-permute-done | bytes 2621472 | tf_op jit(solution)/shard_map/ppermute | solution.py:15
  311.3 1.5 fusion.22
  312.8 1.4 pad_select_fusion.6
  314.2 1.8 pad_select_fusion.5
  316.0 1.8 pad_select_fusion.4
  317.8 1.8 pad_select_fusion.3
  319.6 1.8 pad_select_fusion.2
  321.3 1.8 pad_select_fusion.1
  324.7 1.6 fusion.53
  328.4 22.6 %multiply_reduce_fusion = f32[8192,3]{0,1:T(4,128)S(1)} fusion(f32[8192,256]{0,1:T(8,128)} %fusion.20, f32[512,3,256]{0,2,1:T(8,128)S(1)} %copy.14, s32[8192]{0:T(1024)S(1)} %get-tuple-element.78), kind=kOutput, calls=%fused_computation.14 | convolution fusion | flops 38671458304 | bytes 10092544 | tf_op jit(solution)/shard_map/dot_general | solution.py:147
  351.7 25.2 %fusion.9 = f32[512,3,256]{2,0,1:T(8,128)S(1)} fusion(f32[8192,3]{0,1:T(4,128)S(1)} %get-tuple-element.74, f32[8192,256]{0,1:T(8,128)} %fusion.20, s32[8192]{0:T(1024)S(1)} %get-tuple-element.78), kind=kOutput, calls=%fused_computation.11 | convolution fusion | flops 38665191424 | bytes 10092544 | tf_op jit(solution)/shard_map/dot_general | solution.py:157
  376.9 2.9 constant_dynamic-update-slice_fusion.1
  379.8 1.9 constant_dynamic-update-slice_fusion
  381.7 1.9 fusion.47
  383.6 1.9 fusion.46
  385.6 3.9 fusion.55
  389.5 2.3 copy.18
  391.8 1.5 copy.16
  393.3 2.0 collective-permute-start.6
  395.3 1.9 fusion.54
  398.4 3.7 collective-permute-start.4
  402.2 1.7 copy.19
  403.9 2.9 copy.17
  406.8 6.4 %minimum_multiply_fusion = f32[5,32,16,258]{3,2,1,0:T(8,128)S(1)} fusion(f32[7,32,16,2]{3,2,1,0:T(8,128)S(1)} %copy.19, f32[7,32,16,256]{3,2,1,0:T(8,128)} %fusion.46, f32[7,32,16,2]{3,2,1,0:T(8,128)} %copy.17), kind=kLoop, calls=%fused_computation.54 | loop fusion | flops 9246720 | bytes 6369280 | tf_op jit(solution)/shard_map/mul | solution.py:37
  413.7 2.7 multiply_subtract_fusion
  417.4 3.0 minimum_multiply_fusion.1
  420.5 2.4 multiply_subtract_fusion.1
  423.0 2.5 fusion.37
  (67 shorter events, 9.0 us)
Async XLA Ops:
  0.6 63.1 %collective-permute-start = (f32[5,32,16,256]{3,2,1,0:T(8,128)}, f32[5,32,16,256]{3,2,1,0:T(8,128)S(1)}, u32[]{:S(2)}, u32[]{:S(2)}) collective-permute-start(f32[5,32,16,256]{3,2,1,0:T(8,128)} %param.9), channel_id=1, source_target_pairs={{7,0},{0,1},{1,2},{2,3},{3,4},{4,5},{5,6},{6,7},{15,8},{8,9},{9,10... | collective-permute-start | bytes 7864328 | tf_op jit(solution)/shard_map/ppermute | solution.py:15
  63.8 2.3 copy-start.8
  63.8 2.3 copy-start.9
  65.9 17.3 %copy-start.3 = (f32[5,32,16,256]{3,2,1,0:T(8,128)}, f32[5,32,16,256]{3,2,1,0:T(8,128)S(1)}, u32[]{:S(2)}) copy-start(f32[5,32,16,256]{3,2,1,0:T(8,128)S(1)} %broadcast_select_fusion) | copy-start | bytes 7864324
  65.9 60.0 %collective-permute-start.1 = (f32[5,32,16,256]{3,2,1,0:T(8,128)S(1)}, f32[5,32,16,256]{3,2,1,0:T(8,128)}, u32[]{:S(2)}, u32[]{:S(2)}) collective-permute-start(f32[5,32,16,256]{3,2,1,0:T(8,128)S(1)} %broadcast_select_fusion), channel_id=1, source_target_pairs={{6,0},{7,1},{0,2},{1,3},{2,4},{3,5},{4,6},{5,7},{14,8},{15,9},{8,1... | collective-permute-start | bytes 7864328 | tf_op jit(solution)/shard_map/ppermute | solution.py:15
  66.1 17.2 %copy-start.7 = (f32[3,4096]{1,0:T(4,128)S(1)}, f32[3,4096]{1,0:T(4,128)}, u32[]{:S(2)}) copy-start(f32[3,4096]{1,0:T(4,128)} %param.11) | copy-start | bytes 147460
  66.1 17.2 %copy-start.10 = (f32[4096]{0:T(1024)S(1)}, f32[4096]{0:T(1024)}, u32[]{:S(2)}) copy-start(f32[4096]{0:T(1024)} %param.13) | copy-start | bytes 49156
  66.1 17.2 %copy-start.11 = (f32[4096]{0:T(1024)S(1)}, f32[4096]{0:T(1024)}, u32[]{:S(2)}) copy-start(f32[4096]{0:T(1024)} %param.12) | copy-start | bytes 49156
  128.8 117.5 %collective-permute-start.2 = (f32[5,32,16,256]{3,2,1,0:T(8,128)S(1)}, f32[5,32,16,256]{3,2,1,0:T(8,128)}, u32[]{:S(2)}, u32[]{:S(2)}) collective-permute-start(f32[5,32,16,256]{3,2,1,0:T(8,128)S(1)} %broadcast_select_fusion.1), channel_id=1, source_target_pairs={{4,0},{5,1},{6,2},{7,3},{0,4},{1,5},{2,6},{3,7},{12,8},{13,9},{14,... | collective-permute-start | bytes 7864328 | tf_op jit(solution)/shard_map/ppermute | solution.py:15
  184.5 61.8 %all-to-all-start = ((f32[6,32,256]{2,0,1:T(8,128)}), f32[6,32,256]{2,0,1:T(8,128)S(1)}, u32[]{:S(2)}, u32[]{:S(2)}) async-start(f32[6,32,256]{2,0,1:T(8,128)} %bitcast.6), calls=%async_computation | async-start | bytes 524288 | tf_op jit(solution)/shard_map/all_to_all | solution.py:131
  246.3 5.3 %copy-start.6 = (f32[6,32,256]{2,0,1:T(8,128)}, f32[6,32,256]{2,0,1:T(8,128)S(1)}, u32[]{:S(2)}) copy-start(f32[6,32,256]{2,0,1:T(8,128)S(1)} %all-to-all-done) | copy-start | bytes 589828
  248.4 62.1 %collective-permute-start.3 = (f32[5,32,16,256]{3,2,1,0:T(8,128)S(1)}, f32[5,32,16,256]{3,2,1,0:T(8,128)S(1)}, u32[]{:S(2)}, u32[]{:S(2)}) collective-permute-start(f32[5,32,16,256]{3,2,1,0:T(8,128)S(1)} %broadcast_select_fusion.2), channel_id=1, source_target_pairs={{7,0},{0,1},{1,2},{2,3},{3,4},{4,5},{5,6},{6,7},{15,8},{8,9},{9,10... | collective-permute-start | bytes 7864328 | tf_op jit(solution)/shard_map/ppermute | solution.py:15
  324.7 2.9 copy-start.2
  328.4 22.6 %slice-start = ((f32[6,32,256]{2,0,1:T(8,128)}), f32[3,32,256]{2,0,1:T(4,128)S(1)}, s32[]{:S(2)}) async-start(f32[6,32,256]{2,0,1:T(8,128)} %copy-done.6), calls=%async_computation.1 | async-start | bytes 262144 | tf_op jit(solution)/shard_map/slice | solution.py:151
  391.8 10.4 %collective-permute-start.7 = (f32[7,32,16,2]{1,2,3,0:T(8,128)S(1)}, f32[7,32,16,2]{1,2,3,0:T(8,128)}, u32[]{:S(2)}, u32[]{:S(2)}) collective-permute-start(f32[7,32,16,2]{1,2,3,0:T(8,128)S(1)} %copy.18), channel_id=1, source_target_pairs={{1,0},{2,1},{3,2},{4,3},{5,4},{6,5},{7,6},{0,7},{9,8},{10,9},{11,1... | collective-permute-start | bytes 86024 | tf_op jit(solution)/shard_map/ppermute | solution.py:28
  393.3 10.7 %collective-permute-start.6 = (f32[7,32,16,2]{1,2,3,0:T(8,128)}, f32[7,32,16,2]{1,2,3,0:T(8,128)}, u32[]{:S(2)}, u32[]{:S(2)}) collective-permute-start(f32[7,32,16,2]{1,2,3,0:T(8,128)} %copy.16), channel_id=1, source_target_pairs={{0,1},{1,2},{2,3},{3,4},{4,5},{5,6},{6,7},{7,0},{8,9},{9,10},{10,1... | collective-permute-start | bytes 86024 | tf_op jit(solution)/shard_map/ppermute | solution.py:26
  397.2 19.3 %collective-permute-start.5 = (f32[7,2,16,256]{3,2,1,0:T(8,128)}, f32[7,2,16,256]{3,2,1,0:T(8,128)}, u32[]{:S(2)}, u32[]{:S(2)}) collective-permute-start(f32[7,2,16,256]{3,2,1,0:T(8,128)} %get-tuple-element.70), channel_id=1, source_target_pairs={{8,0},{16,8},{24,16},{9,1},{17,9},{25,17},{10,2},{18,10},{26,18},{... | collective-permute-start | bytes 688136 | tf_op jit(solution)/shard_map/ppermute | solution.py:28
  398.4 18.0 %collective-permute-start.4 = (f32[7,2,16,256]{3,2,1,0:T(8,128)}, f32[7,2,16,256]{3,2,1,0:T(8,128)}, u32[]{:S(2)}, u32[]{:S(2)}) collective-permute-start(f32[7,2,16,256]{3,2,1,0:T(8,128)} %get-tuple-element.69), channel_id=1, source_target_pairs={{0,8},{8,16},{16,24},{1,9},{9,17},{17,25},{2,10},{10,18},{18,26},{... | collective-permute-start | bytes 688136 | tf_op jit(solution)/shard_map/ppermute | solution.py:26
  406.8 6.4 %copy-start = (f32[7,32,16,256]{3,2,1,0:T(8,128)S(1)}, f32[7,32,16,256]{3,2,1,0:T(8,128)}, u32[]{:S(2)}) copy-start(f32[7,32,16,256]{3,2,1,0:T(8,128)} %fusion.46) | copy-start | bytes 11010052
  406.8 6.5 %copy-start.1 = (f32[7,32,16,2]{3,2,1,0:T(8,128)S(1)}, f32[7,32,16,2]{3,2,1,0:T(8,128)}, u32[]{:S(2)}) copy-start(f32[7,32,16,2]{3,2,1,0:T(8,128)} %copy.17) | copy-start | bytes 86020
  420.5 2.5 copy-start.4
  420.5 2.5 copy-start.5
where the time goes:
time: 434 us; the launch traced here: 426 us
  waiting for transfers between devices  214 us (49%)
  matrix products  120 us (28%)
  other arithmetic  52.1 us (12%)
  local copies, waits for them, and re-layouts  20.2 us (5%)
  starting transfers between devices  17.3 us (4%)
    ppermute x4, waiting for transfers between devices, passed_along(): return lax.ppermute(block, axis, route)  157 us
    all_to_all x1, waiting for transfers between devices, local(): lax.all_to_all(outbox, ('rad', 'sec'), split_axis=1, concat_axis=1, tiled...  57.8 us
    dot_general x8, matrix products, place_block(): jnp.dot(record_block, placing, precision=exact, preferred_element_type=jn...  55.5 us
    dot_general x1, matrix products, local(): jnp.dot(row_hot.T, spread, precision=exact, preferred_element_type=jnp.fl...  25.2 us
    dot_general x1, matrix products, local(): jnp.dot(row_hot, velocity_rows, precision=exact, preferred_element_type=j...  22.6 us
    dot_general x1, matrix products, local(): jnp.dot(earlier, hits.astype(jnp.bfloat16), preferred_element_type=jnp.fl...  17.1 us
    select_n x8, other arithmetic, local(): window = jnp.where(chosen[None, :, None, None], moved, window)  12.7 us
    mul x2, other arithmetic, limited_slope(): 0.5 * (jnp.sign(left_step) + jnp.sign(right_step))  9.45 us
  transfers between devices with their start and end apart: 9, of which 4 were waited for; matrix products, arithmetic and copies ran while one was open for 22% of the time, Pallas kernels for 0%

commit v1 on v0

v1 whole, which is shorter than its diff:
```python
import functools
import jax
import jax.numpy as jnp
from jax import lax
from jax.experimental import pallas as pl
from jax.experimental.pallas import tpu as pltpu
from jax.sharding import PartitionSpec as P

sound_speed = 1.0
radial_rate = 0.2
azimuth_rate = 0.2
MESH = pl.DeviceIdType.MESH
VMEM_LIMIT = 48 * 1024 * 1024
in_vmem = pl.BlockSpec(memory_space=pltpu.VMEM)
in_smem = pl.BlockSpec(memory_space=pltpu.SMEM)


def with_halo(cells, sides, width, closed):
    for axis, dim in sides:
        count = lax.axis_size(axis)
        ends = count if closed else count - 1
        head = lax.slice_in_dim(cells, 0, width, axis=dim)
        tail = lax.slice_in_dim(cells, cells.shape[dim] - width, cells.shape[dim], axis=dim)
        cells = jnp.concatenate(
            [
                lax.ppermute(tail, axis, [(i, (i + 1) % count) for i in range(ends)]),
                cells,
                lax.ppermute(head, axis, [((i + 1) % count, i) for i in range(ends)]),
            ],
            axis=dim,
        )
    return cells


def limited_slope(left_step, right_step):
    return (
        0.5
        * (jnp.sign(left_step) + jnp.sign(right_step))
        * jnp.minimum(jnp.abs(left_step), jnp.abs(right_step))
    )


def plm_divergence(values, speed, along_axis, extent):

    def take_range(source, offset_at, length):
        return lax.slice_in_dim(source, offset_at, offset_at + length, axis=along_axis)

    left_step = take_range(values, 1, extent + 2) - take_range(values, 0, extent + 2)
    right_step = take_range(values, 2, extent + 2) - take_range(values, 1, extent + 2)
    slopes = limited_slope(left_step, right_step)
    centre = take_range(values, 1, extent + 2)
    left_value = take_range(centre, 0, extent + 1) + 0.5 * take_range(slopes, 0, extent + 1)
    right_value = take_range(centre, 1, extent + 1) - 0.5 * take_range(slopes, 1, extent + 1)
    face_speed = 0.5 * (take_range(speed, 1, extent + 1) + take_range(speed, 2, extent + 1))
    face_flux = face_speed * 0.5 * (left_value + right_value) - 0.5 * (
        jnp.abs(face_speed) + sound_speed
    ) * (right_value - left_value)
    return take_range(face_flux, 1, extent) - take_range(face_flux, 0, extent)


def split_terms(x, terms):
    parts = []
    for _ in range(terms):
        part = x.astype(jnp.bfloat16)
        parts.append(part)
        x = x - part.astype(jnp.float32)
    return parts


def pack_kernel(devices, capacity, step, dest_ref, rec_ref, out_ref, acc):
    total = dest_ref.shape[1]
    rows = devices * 8
    upper = (
        lax.broadcasted_iota(jnp.int32, (step, step), 0)
        <= lax.broadcasted_iota(jnp.int32, (step, step), 1)
    ).astype(jnp.float32).astype(jnp.bfloat16)
    acc[...] = jnp.zeros_like(acc)

    def body(i, carry):
        at = pl.ds(pl.multiple_of(i * step, step), step)
        dest = dest_ref[:, at]
        hit = (lax.broadcasted_iota(jnp.int32, (devices, step), 0) == dest).astype(jnp.float32)
        running = (
            jnp.dot(hit.astype(jnp.bfloat16), upper, preferred_element_type=jnp.float32) + carry
        )
        slot = jnp.sum(hit * running, axis=0, keepdims=True).astype(jnp.int32) - 1
        slot_hot = (
            (lax.broadcasted_iota(jnp.int32, (capacity, step), 0) == slot)
            .astype(jnp.float32)
            .astype(jnp.bfloat16)
        )
        hit8 = lax.broadcasted_iota(jnp.int32, (rows, step), 0) // 8 == dest
        rec = rec_ref[:, at]
        for k, part in enumerate(split_terms(rec, 3)):
            tiled = jnp.concatenate([part.astype(jnp.float32)] * devices, axis=0)
            placed = jnp.where(hit8, tiled, 0.0).astype(jnp.bfloat16)
            acc[k * rows : (k + 1) * rows] += lax.dot_general(
                placed, slot_hot, (((1,), (1,)), ((), ())), preferred_element_type=jnp.float32
            )
        return running[:, step - 1 : step]

    lax.fori_loop(0, total // step, body, jnp.zeros((devices, 1), jnp.float32))
    joined = (acc[0:rows] + acc[rows : 2 * rows]) + acc[2 * rows : 3 * rows]
    out_ref[...] = joined.reshape(devices, 8, capacity)


def exchange_kernel(
    slabs,
    sectors,
    shift_ref,
    gas_ref,
    outbox_ref,
    shifted_ref,
    inbox_ref,
    *scratch,
):
    fields, radii, layers, width = gas_ref.shape
    land = scratch[:fields]
    rolled = scratch[fields : 2 * fields]
    send1, recv1, send2, recv2, send3, recv3 = scratch[2 * fields :]
    own = radii // sectors
    devices = slabs * sectors
    rad, sec = lax.axis_index("rad"), lax.axis_index("sec")
    me = rad * sectors + sec

    def place(k):
        peer = lax.rem(me + k, devices)
        return peer, (lax.div(peer, sectors), lax.rem(peer, sectors))

    barrier = pltpu.get_barrier_semaphore()

    def greet(k, _):
        pl.semaphore_signal(barrier, inc=1, device_id=place(k)[1], device_id_type=MESH)
        return 0

    lax.fori_loop(1, devices, greet, 0)
    pl.semaphore_wait(barrier, devices - 1)

    def outward(f, k):
        to = lax.rem(sec + k, sectors)
        return pltpu.make_async_remote_copy(
            src_ref=gas_ref.at[f, pl.ds(to * own, own)],
            dst_ref=land[f].at[sec],
            send_sem=send1.at[f, k],
            recv_sem=recv1.at[f, k],
            device_id=(rad, to),
            device_id_type=MESH,
        )

    def homeward(f, k):
        to = lax.rem(sec + k, sectors)
        return pltpu.make_async_remote_copy(
            src_ref=rolled[f].at[to],
            dst_ref=shifted_ref.at[f, pl.ds(sec * own, own)],
            send_sem=send2.at[f, k],
            recv_sem=recv2.at[f, k],
            device_id=(rad, to),
            device_id_type=MESH,
        )

    def parcel(k):
        peer, where = place(k)
        return pltpu.make_async_remote_copy(
            src_ref=outbox_ref.at[peer],
            dst_ref=inbox_ref.at[me],
            send_sem=send3.at[k],
            recv_sem=recv3.at[k],
            device_id=where,
            device_id_type=MESH,
        )

    def each(first, last, act):
        def body(k, _):
            act(k)
            return 0

        lax.fori_loop(first, last, body, 0)

    for f in range(fields):
        each(1, sectors, lambda k: outward(f, k).start())
    each(1, devices, lambda k: parcel(k).start())
    inbox_ref[me] = outbox_ref[me]
    for f in range(fields):
        land[f][sec] = gas_ref[f, pl.ds(sec * own, own)]
        each(1, sectors, lambda k: outward(f, k).wait_recv())

        def turn(r, _):
            shift = shift_ref[sec * own + r]
            quotient = lax.rem(lax.div(shift, width), sectors)
            rest = lax.rem(shift, width)
            early = lax.broadcasted_iota(jnp.int32, (layers, width), 1) < rest

            def source(t):
                return pltpu.roll(land[f][lax.rem(t - quotient + 2 * sectors, sectors), r], rest, 1)

            def fill(t, before):
                now = source(t)
                rolled[f][t, r] = jnp.where(early, before, now)
                return now

            lax.fori_loop(0, sectors, fill, source(-1))
            return 0

        lax.fori_loop(0, own, turn, 0)
        each(1, sectors, lambda k: homeward(f, k).start())
        shifted_ref[f, pl.ds(sec * own, own)] = rolled[f][sec]
    each(1, devices, lambda k: parcel(k).wait())
    for f in range(fields):
        each(1, sectors, lambda k: outward(f, k).wait_send())
    for f in range(fields):
        each(1, sectors, lambda k: homeward(f, k).wait())


def drag_kernel(step, recv_ref, gas_ref, out_ref, dragged_ref, speeds, acc):
    _, rows, width = gas_ref.shape
    total = recv_ref.shape[1]
    for c in range(3):
        turned = (gas_ref[1 + c] / gas_ref[0]).T
        for k, part in enumerate(split_terms(turned, 2)):
            speeds[c * width : (c + 1) * width, k * rows : (k + 1) * rows] = part
    acc[...] = jnp.zeros_like(acc)

    def body(i, _):
        at = pl.ds(pl.multiple_of(i * step, step), step)
        rec = recv_ref[:, at]
        cell = rec[5:6].astype(jnp.int32)
        row, angle = lax.div(cell, width), lax.rem(cell, width)
        row_hot = (
            (lax.broadcasted_iota(jnp.int32, (rows, step), 0) == row)
            .astype(jnp.float32)
            .astype(jnp.bfloat16)
        )
        picked = jnp.dot(
            speeds[...],
            jnp.concatenate([row_hot, row_hot], axis=0),
            preferred_element_type=jnp.float32,
        )
        angle_hot = lax.broadcasted_iota(jnp.int32, (width, step), 0) == angle
        stop = rec[4:5]
        fraction = stop / (1.0 + stop)
        spread = [[], []]
        for c in range(3):
            local = jnp.sum(
                jnp.where(angle_hot, picked[c * width : (c + 1) * width], 0.0),
                axis=0,
                keepdims=True,
            )
            velocity = rec[c : c + 1]
            change = (velocity - local) * fraction
            out_ref[c : c + 1, at] = velocity - change
            for k, part in enumerate(split_terms(rec[3:4] * change, 2)):
                spread[k].append(
                    jnp.where(angle_hot, part.astype(jnp.float32), 0.0).astype(jnp.bfloat16)
                )
        acc[...] += lax.dot_general(
            jnp.concatenate(spread[0] + spread[1], axis=0),
            row_hot,
            (((1,), (1,)), ((), ())),
            preferred_element_type=jnp.float32,
        )
        return 0

    lax.fori_loop(0, total // step, body, 0)
    dragged_ref[0] = gas_ref[0]
    dragged_ref[4] = gas_ref[4]
    for c in range(3):
        added = (
            acc[c * width : (c + 1) * width] + acc[(3 + c) * width : (4 + c) * width]
        )
        dragged_ref[1 + c] = gas_ref[1 + c] + added.T


def local(
    slabs,
    sectors,
    gas_fields,
    orbit_shift,
    particle_velocity,
    particle_mass,
    particle_stop,
    particle_cell,
    particle_dest,
):
    fields, radii, layers, sector = gas_fields.shape
    per_device = particle_dest.shape[0]
    devices = slabs * sectors
    capacity = 2 * per_device // devices
    own = radii // sectors
    rows = radii * layers
    slots = devices * capacity
    records = jnp.concatenate(
        [
            particle_velocity,
            particle_mass[None],
            particle_stop[None],
            particle_cell[None].astype(jnp.float32),
            jnp.zeros((2, per_device), jnp.float32),
        ],
        axis=0,
    )
    limit = pltpu.CompilerParams(vmem_limit_bytes=VMEM_LIMIT)
    outbox = pl.pallas_call(
        functools.partial(pack_kernel, devices, capacity, 512),
        out_shape=jax.ShapeDtypeStruct((devices, 8, capacity), jnp.float32),
        in_specs=[in_vmem, in_vmem],
        out_specs=in_vmem,
        scratch_shapes=[pltpu.VMEM((3 * devices * 8, capacity), jnp.float32)],
        compiler_params=limit,
    )(particle_dest.reshape(1, per_device), records)
    dma = pltpu.SemaphoreType.DMA
    shifted, inbox = pl.pallas_call(
        functools.partial(exchange_kernel, slabs, sectors),
        out_shape=(
            jax.ShapeDtypeStruct(gas_fields.shape, jnp.float32),
            jax.ShapeDtypeStruct((devices, 8, capacity), jnp.float32),
        ),
        in_specs=[in_smem, in_vmem, in_vmem],
        out_specs=(in_vmem, in_vmem),
        scratch_shapes=[pltpu.VMEM((sectors, own, layers, sector), jnp.float32)] * (2 * fields)
        + [dma((fields, sectors))] * 4
        + [dma((devices,))] * 2,
        compiler_params=pltpu.CompilerParams(
            vmem_limit_bytes=VMEM_LIMIT, collective_id=0, has_side_effects=True
        ),
    )(orbit_shift, gas_fields, outbox)
    received = inbox.transpose(1, 0, 2).reshape(8, slots)
    arrived_velocity, dragged = pl.pallas_call(
        functools.partial(drag_kernel, 512),
        out_shape=(
            jax.ShapeDtypeStruct((3, slots), jnp.float32),
            jax.ShapeDtypeStruct((fields, rows, sector), jnp.float32),
        ),
        in_specs=[in_vmem, in_vmem],
        out_specs=(in_vmem, in_vmem),
        scratch_shapes=[
            pltpu.VMEM((3 * sector, 2 * rows), jnp.bfloat16),
            pltpu.VMEM((6 * sector, rows), jnp.float32),
        ],
        compiler_params=limit,
    )(received, shifted.reshape(fields, rows, sector))
    dragged = dragged.reshape(fields, radii, layers, sector)
    radial_speed = dragged[1] / dragged[0]
    azimuthal_speed = dragged[2] / dragged[0]
    stacked = jnp.concatenate([dragged, radial_speed[None], azimuthal_speed[None]], axis=0)
    radial_pad = with_halo(stacked, (("rad", 1),), 2, False)
    azimuth_pad = with_halo(stacked, (("sec", 3),), 2, True)
    radial_change = plm_divergence(radial_pad[0:5], radial_pad[5:6], 1, radii)
    azimuth_change = plm_divergence(azimuth_pad[0:5], azimuth_pad[6:7], 3, sector)
    gas_next = dragged - radial_rate * radial_change - azimuth_rate * azimuth_change
    return (gas_next, arrived_velocity)


def solution(mesh):
    placed = (
        P(None, "rad", None, "sec"),
        P("rad"),
        P(None, ("rad", "sec")),
        P(("rad", "sec")),
        P(("rad", "sec")),
        P(("rad", "sec")),
        P(("rad", "sec"), None),
    )
    return jax.shard_map(
        functools.partial(local, mesh.shape["rad"], mesh.shape["sec"]),
        mesh=mesh,
        in_specs=placed,
        out_specs=(P(None, "rad", None, "sec"), P(None, ("rad", "sec"))),
        check_vma=False,
    )
```

time: 434 us -> 218 us (0.50); the launches traced: 426 us -> 216 us
  waiting for transfers between devices: 214 us -> 0.01 us
  Pallas kernels: 0 us -> 162 us
  matrix products: 120 us -> 0 us
  other arithmetic: 52.1 us -> 24.9 us
  starting transfers between devices: 17.3 us -> 10.1 us
    pallas_call x0 -> x3, Pallas kernels: none -> 162 us  [the longest x1 126 us: local(): pl.pallas_call(functools.partial(exchange_kernel, slabs, sectors), out_sh...]
    ppermute x4 -> x0, waiting for transfers between devices: 157 us -> none  [passed_along(): return lax.ppermute(block, axis, route)]
    dot_general x11 -> x0, matrix products: 120 us -> none  [the longest x8 55.5 us: place_block(): jnp.dot(record_block, placing, precision=exact, preferred_element_type=jn...]
    all_to_all x1 -> x0, waiting for transfers between devices: 57.8 us -> none  [local(): lax.all_to_all(outbox, ('rad', 'sec'), split_axis=1, concat_axis=1, tiled...]
    select_n x12 -> x0, other arithmetic: 19.9 us -> none  [the longest x8 12.7 us: local(): window = jnp.where(chosen[None, :, None, None], moved, window)]
    ppermute x4 -> x0, starting transfers between devices: 6.26 us -> none  [passed_along(): return lax.ppermute(block, axis, route)]
    concatenate x1 -> x2, other arithmetic: 0.7 us -> 6.85 us  [with_halo(): jnp.concatenate([lax.ppermute(tail, axis, [(i, (i + 1) % count) for i in...]
    unnamed x25 -> x16, local copies, waits for them, and re-layouts: 3.26 us -> 8.76 us
  transfers between devices with their start and end apart: 9 -> 4, of which waited for: 4 -> 0; matrix products, arithmetic and copies ran while one was open for 22% -> 11% of each run, Pallas kernels for 0% -> 0%
where the time goes in v1:
time: 218 us; the launch traced here: 216 us
  Pallas kernels  162 us (74%)
  other arithmetic  24.9 us (11%)
  local copies, waits for them, and re-layouts  18 us (8%)
  starting transfers between devices  10.1 us (5%)
    pallas_call x1, Pallas kernels, local(): pl.pallas_call(functools.partial(exchange_kernel, slabs, sectors), out_sh...  126 us
    pallas_call x1, Pallas kernels, local(): pl.pallas_call(functools.partial(drag_kernel, 512), out_shape=(jax.ShapeD...  31.2 us
    unnamed x16, local copies, waits for them, and re-layouts  8.76 us
    mul x2, other arithmetic, limited_slope(): 0.5 * (jnp.sign(left_step) + jnp.sign(right_step))  7.91 us
    concatenate x2, other arithmetic, with_halo(): jnp.concatenate([lax.ppermute(tail, axis, [(i, (i + 1) % count) for i in...  6.85 us
    ppermute x2, starting transfers between devices, with_halo(): lax.ppermute(head, axis, [((i + 1) % count, i) for i in range(ends)])  5.98 us
    pallas_call x1, Pallas kernels, local(): pl.pallas_call(functools.partial(pack_kernel, devices, capacity, 512), ou...  5.01 us
  transfers between devices with their start and end apart: 4, of which 0 were waited for; matrix products, arithmetic and copies ran while one was open for 11% of the time, Pallas kernels for 0%

profile of v1, /device:TPU:0, one launch (start us, length us, event | category | flops | bytes accessed | tf_op | source)
XLA Modules:
  0.0 215.6 jit_solution(16393100777137960546)
XLA Ops:
  0.6 0.7 convert_element_type.6
  1.4 1.0 concatenate.32.rec_ref
  2.3 0.0 copy-start.1
  2.4 0.7 copy-done.1
  3.1 5.0 %shard_map.86.outbox_ref = f32[32,8,256]{2,1,0:T(8,128)S(1)} custom-call(s32[1,4096]{1,0:T(1,128)S(1)} %bitcast.30, f32[8,4096]{1,0:T(8,128)S(1)} %concatenate.32.rec_ref), custom_call_target="tpu_custom_call" | custom-call | tf_op jit(solution)/shard_map/pallas_call | solution.py:302
  8.1 0.0 copy-start
  8.1 1.7 copy-done
  9.8 0.0 copy-start.2
  9.8 0.7 copy-done.2
  10.5 125.5 %shard_map.87 = (f32[5,32,16,256]{3,2,1,0:T(8,128)S(1)}, f32[32,8,256]{2,1,0:T(8,128)S(1)}) custom-call(s32[32]{0:T(128)S(1)} %copy-done.2, f32[5,32,16,256]{3,2,1,0:T(8,128)S(1)} %copy-done, f32[32,8,256]{2,1,0:T(8,128)S(1)} %shard_map.86.outbox_ref), custom_call_target="tpu_custom_call" | custom-call | tf_op jit(solution)/shard_map/pallas_call | solution.py:311
  136.0 31.2 %shard_map.88 = (f32[3,8192]{1,0:T(4,128)}, f32[5,512,256]{2,1,0:T(8,128)S(1)}) custom-call(f32[8,8192]{1,0:T(8,128)S(1)} %bitcast.29, f32[5,512,256]{2,1,0:T(8,128)S(1)} %bitcast.28), custom_call_target="tpu_custom_call" | custom-call | tf_op jit(solution)/shard_map/pallas_call | solution.py:327
  167.2 0.1 slice_divide_fusion.1
  167.3 0.0 copy-start.3
  167.3 0.4 pad_maximum_fusion.6
  167.7 0.4 copy-done.3
  168.2 2.5 %fusion.8 = (f32[7,32,16,2]{3,2,1,0:T(8,128)}, f32[7,32,16,2]{3,2,1,0:T(8,128)}) fusion(f32[7,32,16,256]{3,2,1,0:T(8,128)S(1)} %pad_maximum_fusion.6), kind=kLoop, calls=%fused_computation.45 | loop fusion | bytes 114688 | tf_op jit(solution)/shard_map/slice | solution.py:23
  170.7 2.3 %copy.20 = f32[7,32,16,2]{1,2,3,0:T(8,128)S(1)} copy(f32[7,32,16,2]{3,2,1,0:T(8,128)} %get-tuple-element.22) | data formatting | bytes 57344
  173.0 2.8 %collective-permute-start.2 = (f32[7,32,16,2]{1,2,3,0:T(8,128)S(1)}, f32[7,32,16,2]{1,2,3,0:T(8,128)}, u32[]{:S(2)}, u32[]{:S(2)}) collective-permute-start(f32[7,32,16,2]{1,2,3,0:T(8,128)S(1)} %copy.20), channel_id=1, source_target_pairs={{0,1},{1,2},{2,3},{3,4},{4,5},{5,6},{6,7},{7,0},{8,9},{9,10},{10,1... | collective-permute-start | bytes 86024 | tf_op jit(solution)/shard_map/ppermute | solution.py:26
  175.8 2.9 %copy.21 = f32[7,32,16,2]{1,2,3,0:T(8,128)} copy(f32[7,32,16,2]{3,2,1,0:T(8,128)} %get-tuple-element.23) | data formatting | bytes 57344
  178.7 4.5 %collective-permute-start.3 = (f32[7,32,16,2]{1,2,3,0:T(8,128)}, f32[7,32,16,2]{1,2,3,0:T(8,128)}, u32[]{:S(2)}, u32[]{:S(2)}) collective-permute-start(f32[7,32,16,2]{1,2,3,0:T(8,128)} %copy.21), channel_id=1, source_target_pairs={{1,0},{2,1},{3,2},{4,3},{5,4},{6,5},{7,6},{0,7},{9,8},{10,9},{11,1... | collective-permute-start | bytes 86024 | tf_op jit(solution)/shard_map/ppermute | solution.py:28
  183.2 1.6 pad_maximum_fusion.12
  184.8 1.4 collective-permute-start
  186.1 1.5 collective-permute-start.1
  187.6 0.0 collective-permute-done.2
  187.6 2.9 %copy.15 = f32[7,32,16,2]{3,2,1,0:T(8,128)} copy(f32[7,32,16,2]{1,2,3,0:T(8,128)} %collective-permute-done.2) | data formatting | bytes 57344 | tf_op jit(solution)/shard_map/ppermute | solution.py:26
  190.5 0.0 collective-permute-done.3
  190.5 2.9 %copy.17 = f32[7,32,16,2]{3,2,1,0:T(8,128)} copy(f32[7,32,16,2]{1,2,3,0:T(8,128)} %collective-permute-done.3) | data formatting | bytes 57344 | tf_op jit(solution)/shard_map/ppermute | solution.py:28
  193.4 0.0 copy-start.4
  193.4 0.0 copy-start.5
  193.4 0.0 copy-start.6
  193.4 4.9 %maximum_maximum_fusion = (f32[7,32,16,258]{3,2,1,0:T(8,128)S(1)}, f32[7,32,16,258]{3,2,1,0:T(8,128)S(1)}) fusion(f32[1,32,16,256]{3,2,1,0:T(8,128)} %bitcast.41, f32[1,32,16,256]{3,2,1,0:T(8,128)S(1)} %bitcast.33, f32[5,32,16,256]{3,2,1,0:T(8,128)S(1)} %bitcast.21, f32[7,32,16,2]{3,2,1,0:T(8,128)} %copy.15, f32[7,32,16,2]{3,2,1,0:T(8,128)} %copy.17), kind=kLoop, calls=%fused_computation | loop fusion | flops 5548032 | bytes 11124736 | tf_op jit(solution)/shard_map/concatenate | solution.py:24
  198.3 0.0 copy-done.4
  198.3 0.0 copy-done.5
  198.4 0.0 copy-done.6
  198.4 0.3 multiply_bitcast_fusion.1
  198.7 0.1 multiply_bitcast_fusion
  198.8 5.1 %minimum_multiply_fusion = f32[5,32,16,258]{3,2,1,0:T(8,128)S(1)} fusion(f32[7,32,16,258]{3,2,1,0:T(8,128)S(1)} %get-tuple-element.21, f32[7,32,16,258]{3,2,1,0:T(8,128)S(1)} %get-tuple-element.20, f32[7,32,16,2]{3,2,1,0:T(8,128)S(1)} %copy-done.6, f32[1,32,16,256]{3,2,1,0:T(8,128)S(1)} %bitcast.43, f32[1,32,16,256]{3,2,1,0:T(8,128)S(1)} %bitcast.35, ...), kind=kLoop, calls=%fused_computation.13 | loop fusion | flops 9246720 | bytes 11653120 | tf_op jit(solution)/shard_map/mul | solution.py:37
  204.0 2.2 %multiply_subtract_fusion = f32[5,32,16,257]{3,2,1,0:T(8,128)S(1)} fusion(f32[5,32,16,258]{3,2,1,0:T(8,128)S(1)} %minimum_multiply_fusion, f32[7,32,16,258]{3,2,1,0:T(8,128)S(1)} %get-tuple-element.20, f32[7,32,16,258]{3,2,1,0:T(8,128)S(1)} %get-tuple-element.21, f32[32,16,257]{2,1,0:T(8,128)S(1)} %multiply_bitcast_fusion, ...), kind=kLoop, calls=%fused_computation.12 | loop fusion | flops 5921280 | bytes 14211072 | tf_op jit(solution)/shard_map/sub | solution.py:55
  206.2 0.0 collective-permute-done
  206.2 0.0 collective-permute-done.1
  206.2 0.8 multiply_bitcast_fusion.3
  207.0 0.1 multiply_bitcast_fusion.2
  207.1 1.9 maximum_maximum_fusion.1
  209.0 2.8 %minimum_multiply_fusion.1 = f32[5,34,16,256]{3,2,1,0:T(8,128)S(1)} fusion(f32[7,34,16,256]{3,2,1,0:T(8,128)S(1)} %get-tuple-element.17, f32[7,34,16,256]{3,2,1,0:T(8,128)S(1)} %get-tuple-element.16, f32[7,2,16,256]{3,2,1,0:T(8,128)} %collective-permute-done.1, f32[1,32,16,256]{3,2,1,0:T(8,128)S(1)} %bitcast.46, f32[1,32,16,256]{3,2,1,0:T(8,128)S(1)} %bitcast.38, ...), kind=kLoop, calls=%fused_computation.23 | loop fusion | flops 9748480 | bytes 12484608 | tf_op jit(solution)/shard_map/mul | solution.py:37
  211.9 1.2 multiply_subtract_fusion.1
  213.0 2.5 %fusion.5 = f32[5,32,16,256]{3,2,1,0:T(8,128)} fusion(f32[5,32,16,257]{3,2,1,0:T(8,128)S(1)} %multiply_subtract_fusion, f32[5,32,16,256]{3,2,1,0:T(8,128)S(1)} %bitcast.27, f32[5,33,16,256]{3,2,1,0:T(8,128)S(1)} %multiply_subtract_fusion.1), kind=kLoop, calls=%fused_computation.31 | loop fusion | flops 3932160 | bytes 15728640 | tf_op jit(solution)/shard_map/sub | solution.py:349
  (1 shorter events, 0.0 us)
Async XLA Ops:
  2.3 0.7 copy-start.1
  8.1 1.7 copy-start
  9.8 0.7 copy-start.2
  167.3 0.9 copy-start.3
  173.0 14.7 %collective-permute-start.2 = (f32[7,32,16,2]{1,2,3,0:T(8,128)S(1)}, f32[7,32,16,2]{1,2,3,0:T(8,128)}, u32[]{:S(2)}, u32[]{:S(2)}) collective-permute-start(f32[7,32,16,2]{1,2,3,0:T(8,128)S(1)} %copy.20), channel_id=1, source_target_pairs={{0,1},{1,2},{2,3},{3,4},{4,5},{5,6},{6,7},{7,0},{8,9},{9,10},{10,1... | collective-permute-start | bytes 86024 | tf_op jit(solution)/shard_map/ppermute | solution.py:26
  178.7 11.8 %collective-permute-start.3 = (f32[7,32,16,2]{1,2,3,0:T(8,128)}, f32[7,32,16,2]{1,2,3,0:T(8,128)}, u32[]{:S(2)}, u32[]{:S(2)}) collective-permute-start(f32[7,32,16,2]{1,2,3,0:T(8,128)} %copy.21), channel_id=1, source_target_pairs={{1,0},{2,1},{3,2},{4,3},{5,4},{6,5},{7,6},{0,7},{9,8},{10,9},{11,1... | collective-permute-start | bytes 86024 | tf_op jit(solution)/shard_map/ppermute | solution.py:28
  184.8 21.4 %collective-permute-start = (f32[7,2,16,256]{3,2,1,0:T(8,128)}, f32[7,2,16,256]{3,2,1,0:T(8,128)S(1)}, u32[]{:S(2)}, u32[]{:S(2)}) collective-permute-start(f32[7,2,16,256]{3,2,1,0:T(8,128)} %get-tuple-element.18), channel_id=1, source_target_pairs={{0,8},{8,16},{16,24},{1,9},{9,17},{17,25},{2,10},{10,18},{18,26},{... | collective-permute-start | bytes 688136 | tf_op jit(solution)/shard_map/ppermute | solution.py:26
  186.1 20.1 %collective-permute-start.1 = (f32[7,2,16,256]{3,2,1,0:T(8,128)}, f32[7,2,16,256]{3,2,1,0:T(8,128)}, u32[]{:S(2)}, u32[]{:S(2)}) collective-permute-start(f32[7,2,16,256]{3,2,1,0:T(8,128)} %get-tuple-element.19), channel_id=1, source_target_pairs={{8,0},{16,8},{24,16},{9,1},{17,9},{25,17},{10,2},{18,10},{26,18},{... | collective-permute-start | bytes 688136 | tf_op jit(solution)/shard_map/ppermute | solution.py:28
  193.4 4.9 %copy-start.4 = (f32[1,512,256]{2,1,0:T(8,128)S(1)}, f32[1,512,256]{2,1,0:T(8,128)}, u32[]{:S(2)}) copy-start(f32[1,512,256]{2,1,0:T(8,128)} %copy-done.3) | copy-start | bytes 1572868
  193.4 5.0 %copy-start.5 = (f32[7,32,16,2]{3,2,1,0:T(8,128)S(1)}, f32[7,32,16,2]{3,2,1,0:T(8,128)}, u32[]{:S(2)}) copy-start(f32[7,32,16,2]{3,2,1,0:T(8,128)} %copy.15) | copy-start | bytes 86020
  193.4 5.0 %copy-start.6 = (f32[7,32,16,2]{3,2,1,0:T(8,128)S(1)}, f32[7,32,16,2]{3,2,1,0:T(8,128)}, u32[]{:S(2)}) copy-start(f32[7,32,16,2]{3,2,1,0:T(8,128)} %copy.17) | copy-start | bytes 86020

commit v2 on v1

v2 whole, which is shorter than its diff:
```python
import functools
import jax
import jax.numpy as jnp
from jax import lax
from jax.experimental import pallas as pl
from jax.experimental.pallas import tpu as pltpu
from jax.sharding import PartitionSpec as P

sound_speed = 1.0
radial_rate = 0.2
azimuth_rate = 0.2
MESH = pl.DeviceIdType.MESH
VMEM_LIMIT = 48 * 1024 * 1024
in_vmem = pl.BlockSpec(memory_space=pltpu.VMEM)
in_smem = pl.BlockSpec(memory_space=pltpu.SMEM)


def limited_slope(left_step, right_step):
    rising = jnp.maximum(jnp.minimum(left_step, right_step), 0.0)
    return rising + jnp.minimum(jnp.maximum(left_step, right_step), 0.0)


def face_flux(left_value, right_value, left_speed, right_speed):
    face_speed = 0.5 * (left_speed + right_speed)
    return face_speed * 0.5 * (left_value + right_value) - 0.5 * (
        jnp.abs(face_speed) + sound_speed
    ) * (right_value - left_value)


def leading_divergence(values, speed, extent):
    steps = values[1:] - values[:-1]
    slopes = 0.5 * limited_slope(steps[:-1], steps[1:])
    centre = values[1:-1]
    flux = face_flux(
        centre[:-1] + slopes[:-1],
        centre[1:] - slopes[1:],
        speed[1 : extent + 2],
        speed[2 : extent + 3],
    )
    return flux[1:] - flux[:-1]


def lane_divergence(values, speed, far_left, left, right, far_right, left_speed, right_speed):
    width = values.shape[1]
    lane = lax.broadcasted_iota(jnp.int32, values.shape, 1)
    first, last = lane == 0, lane == width - 1

    def after(x, end):
        return jnp.where(last, end, pltpu.roll(x, width - 1, 1))

    def before(x, start):
        return jnp.where(first, start, pltpu.roll(x, 1, 1))

    head, tail = values[:, 0:1], values[:, width - 1 : width]
    following = after(values, right)
    step = following - values
    slopes = 0.5 * limited_slope(before(step, head - left), step)
    end_slope = 0.5 * limited_slope(right - tail, far_right - right)
    start_slope = 0.5 * limited_slope(left - far_left, head - left)
    flux = face_flux(
        values + slopes,
        following - after(slopes, end_slope),
        speed,
        after(speed, right_speed),
    )
    start_flux = face_flux(
        left + start_slope, head - slopes[:, 0:1], left_speed, speed[:, 0:1]
    )
    return flux - before(flux, start_flux)


def split_terms(x, terms):
    parts = []
    for _ in range(terms):
        part = x.astype(jnp.bfloat16)
        parts.append(part)
        x = x - part.astype(jnp.float32)
    return parts


def pack_kernel(devices, capacity, step, dest_ref, rec_ref, out_ref, acc):
    total = dest_ref.shape[1]
    rows = devices * 8
    upper = (
        lax.broadcasted_iota(jnp.int32, (step, step), 0)
        <= lax.broadcasted_iota(jnp.int32, (step, step), 1)
    ).astype(jnp.float32).astype(jnp.bfloat16)
    acc[...] = jnp.zeros_like(acc)

    def body(i, carry):
        at = pl.ds(pl.multiple_of(i * step, step), step)
        dest = dest_ref[:, at]
        hit = (lax.broadcasted_iota(jnp.int32, (devices, step), 0) == dest).astype(jnp.float32)
        running = (
            jnp.dot(hit.astype(jnp.bfloat16), upper, preferred_element_type=jnp.float32) + carry
        )
        slot = jnp.sum(hit * running, axis=0, keepdims=True).astype(jnp.int32) - 1
        slot_hot = (
            (lax.broadcasted_iota(jnp.int32, (capacity, step), 0) == slot)
            .astype(jnp.float32)
            .astype(jnp.bfloat16)
        )
        hit8 = lax.broadcasted_iota(jnp.int32, (rows, step), 0) // 8 == dest
        rec = rec_ref[:, at]
        for k, part in enumerate(split_terms(rec, 3)):
            tiled = jnp.concatenate([part.astype(jnp.float32)] * devices, axis=0)
            placed = jnp.where(hit8, tiled, 0.0).astype(jnp.bfloat16)
            acc[k * rows : (k + 1) * rows] += lax.dot_general(
                placed, slot_hot, (((1,), (1,)), ((), ())), preferred_element_type=jnp.float32
            )
        return running[:, step - 1 : step]

    lax.fori_loop(0, total // step, body, jnp.zeros((devices, 1), jnp.float32))
    joined = (acc[0:rows] + acc[rows : 2 * rows]) + acc[2 * rows : 3 * rows]
    out_ref[...] = joined.reshape(devices, 8, capacity)


def step_kernel(
    slabs,
    sectors,
    step,
    shift_ref,
    gas_ref,
    dest_ref,
    rec_ref,
    padded_ref,
    out_ref,
    low_ref,
    high_ref,
    *scratch,
):
    fields, radii, layers, width = gas_ref.shape
    land = scratch[:fields]
    rolled = scratch[fields : 2 * fields]
    outbox, inbox, pack_acc, speeds, acc, low_edge, high_edge = scratch[2 * fields : 2 * fields + 7]
    send1, recv1, send2, recv2, send3, recv3, send4, recv4 = scratch[2 * fields + 7 :]
    own = radii // sectors
    rows = radii * layers
    devices = slabs * sectors
    capacity = outbox.shape[2]
    rad, sec = lax.axis_index("rad"), lax.axis_index("sec")
    me = rad * sectors + sec

    def place(k):
        peer = lax.rem(me + k, devices)
        return peer, (lax.div(peer, sectors), lax.rem(peer, sectors))

    barrier = pltpu.get_barrier_semaphore()

    def greet(k, _):
        pl.semaphore_signal(barrier, inc=1, device_id=place(k)[1], device_id_type=MESH)
        return 0

    lax.fori_loop(1, devices, greet, 0)
    pl.semaphore_wait(barrier, devices - 1)

    def outward(f, k):
        to = lax.rem(sec + k, sectors)
        return pltpu.make_async_remote_copy(
            src_ref=gas_ref.at[f, pl.ds(to * own, own)],
            dst_ref=land[f].at[sec],
            send_sem=send1.at[f, k],
            recv_sem=recv1.at[f, k],
            device_id=(rad, to),
            device_id_type=MESH,
        )

    def homeward(f, k):
        to = lax.rem(sec + k, sectors)
        return pltpu.make_async_remote_copy(
            src_ref=rolled[f].at[to],
            dst_ref=padded_ref.at[f, pl.ds(2 + sec * own, own)],
            send_sem=send2.at[f, k],
            recv_sem=recv2.at[f, k],
            device_id=(rad, to),
            device_id_type=MESH,
        )

    def parcel(k):
        peer, where = place(k)
        return pltpu.make_async_remote_copy(
            src_ref=outbox.at[peer],
            dst_ref=inbox.at[me],
            send_sem=send3.at[k],
            recv_sem=recv3.at[k],
            device_id=where,
            device_id_type=MESH,
        )

    def each(first, last, act):
        def body(k, _):
            act(k)
            return 0

        lax.fori_loop(first, last, body, 0)

    def turn_field(f):
        land[f][sec] = gas_ref[f, pl.ds(sec * own, own)]
        each(1, sectors, lambda k: outward(f, k).wait_recv())

        def turn(r, _):
            shift = shift_ref[sec * own + r]
            quotient = lax.rem(lax.div(shift, width), sectors)
            rest = lax.rem(shift, width)
            early = lax.broadcasted_iota(jnp.int32, (layers, width), 1) < rest

            def source(t):
                return pltpu.roll(land[f][lax.rem(t - quotient + 2 * sectors, sectors), r], rest, 1)

            def fill(t, before):
                now = source(t)
                rolled[f][t, r] = jnp.where(early, before, now)
                return now

            lax.fori_loop(0, sectors, fill, source(-1))
            return 0

        lax.fori_loop(0, own, turn, 0)
        each(1, sectors, lambda k: homeward(f, k).start())
        padded_ref[f, pl.ds(2 + sec * own, own)] = rolled[f][sec]

    def field(f):
        return padded_ref[f, 2 : 2 + radii].reshape(rows, width)

    energy = fields - 1
    for f in range(energy):
        each(1, sectors, lambda k: outward(f, k).start())
    pack_kernel(devices, capacity, step, dest_ref, rec_ref, outbox, pack_acc)
    each(1, devices, lambda k: parcel(k).start())
    inbox[me] = outbox[me]
    for f in range(energy):
        turn_field(f)
    for f in range(energy):
        if f == energy - 1:
            each(1, sectors, lambda k: outward(energy, k).start())
        each(1, sectors, lambda k: homeward(f, k).wait_recv())
    each(1, devices, lambda k: parcel(k).wait())

    for c in range(3):
        turned = (field(1 + c) / field(0)).T
        for k, part in enumerate(split_terms(turned, 2)):
            speeds[c * width : (c + 1) * width, k * rows : (k + 1) * rows] = part
    acc[...] = jnp.zeros_like(acc)
    group = step // capacity

    def drag(i, _):
        at = pl.ds(pl.multiple_of(i * step, step), step)
        rec = jnp.concatenate([inbox[i * group + j] for j in range(group)], axis=1)
        cell = rec[5:6].astype(jnp.int32)
        row, angle = lax.div(cell, width), lax.rem(cell, width)
        row_hot = (
            (lax.broadcasted_iota(jnp.int32, (rows, step), 0) == row)
            .astype(jnp.float32)
            .astype(jnp.bfloat16)
        )
        picked = jnp.dot(
            speeds[...],
            jnp.concatenate([row_hot, row_hot], axis=0),
            preferred_element_type=jnp.float32,
        )
        angle_hot = lax.broadcasted_iota(jnp.int32, (width, step), 0) == angle
        stop = rec[4:5]
        fraction = stop / (1.0 + stop)
        spread = [[], []]
        for c in range(3):
            local_speed = jnp.sum(
                jnp.where(angle_hot, picked[c * width : (c + 1) * width], 0.0),
                axis=0,
                keepdims=True,
            )
            velocity = rec[c : c + 1]
            change = (velocity - local_speed) * fraction
            out_ref[c : c + 1, at] = velocity - change
            for k, part in enumerate(split_terms(rec[3:4] * change, 2)):
                spread[k].append(
                    jnp.where(angle_hot, part.astype(jnp.float32), 0.0).astype(jnp.bfloat16)
                )
        acc[...] += lax.dot_general(
            jnp.concatenate(spread[0] + spread[1], axis=0),
            row_hot,
            (((1,), (1,)), ((), ())),
            preferred_element_type=jnp.float32,
        )
        return 0

    blocks = devices * capacity // step
    lax.fori_loop(0, blocks // 2, drag, 0)
    turn_field(energy)
    lax.fori_loop(blocks // 2, blocks, drag, 0)
    for c in range(3):
        added = acc[c * width : (c + 1) * width] + acc[(3 + c) * width : (4 + c) * width]
        total = field(1 + c) + added.T
        padded_ref[1 + c, 2 : 2 + radii] = total.reshape(radii, layers, width)
    each(1, sectors, lambda k: homeward(energy, k).wait_recv())

    for f in range(fields):
        whole = field(f)
        low_edge[f] = whole[:, 0:128].T[0:8]
        high_edge[f] = whole[:, width - 128 : width].T[120:128]
    up, down = lax.rem(rad + 1, slabs), lax.rem(rad + slabs - 1, slabs)
    east, west = lax.rem(sec + 1, sectors), lax.rem(sec + sectors - 1, sectors)
    halos = []
    for n, (src, dst, where) in enumerate(
        [
            (padded_ref.at[:, 2:4], padded_ref.at[:, 2 + radii : 4 + radii], (down, sec)),
            (padded_ref.at[:, radii : 2 + radii], padded_ref.at[:, 0:2], (up, sec)),
            (low_edge, high_ref, (rad, west)),
            (high_edge, low_ref, (rad, east)),
        ]
    ):
        halos.append(
            pltpu.make_async_remote_copy(
                src_ref=src,
                dst_ref=dst,
                send_sem=send4.at[n],
                recv_sem=recv4.at[n],
                device_id=where,
                device_id_type=MESH,
            )
        )
    for copy in halos:
        copy.start()
    for f in range(fields):
        each(1, sectors, lambda k: outward(f, k).wait_send())
        each(1, sectors, lambda k: homeward(f, k).wait_send())
    for copy in halos:
        copy.wait()

    @pl.when(rad == 0)
    def _():
        padded_ref[:, 0:2] = jnp.zeros((fields, 2, layers, width), jnp.float32)

    @pl.when(rad == slabs - 1)
    def _():
        padded_ref[:, 2 + radii : 4 + radii] = jnp.zeros((fields, 2, layers, width), jnp.float32)


def transport_kernel(chunk, padded_ref, low_ref, high_ref, next_ref, sides):
    fields, radii, layers, width = next_ref.shape
    rows = chunk * layers
    for f in range(fields):
        sides[f] = jnp.concatenate([high_ref[f], low_ref[f]] * 8, axis=0).T

    def body(i, _):
        r = i * chunk
        density = padded_ref[0, pl.ds(r, chunk + 4)]
        density = jnp.where(density == 0.0, 1.0, density)
        radial_speed = padded_ref[1, pl.ds(r, chunk + 4)] / density
        speed = (padded_ref[2, pl.ds(r + 2, chunk)] / density[2 : 2 + chunk]).reshape(rows, width)
        at = pl.ds(pl.multiple_of(r * layers, rows), rows)
        end_speed = sides[2, at] / sides[0, at]
        for f in range(fields):
            values = padded_ref[f, pl.ds(r, chunk + 4)]
            centre = values[2 : 2 + chunk]
            side = sides[f, at]
            along = lane_divergence(
                centre.reshape(rows, width),
                speed,
                side[:, 14:15],
                side[:, 15:16],
                side[:, 0:1],
                side[:, 1:2],
                end_speed[:, 15:16],
                end_speed[:, 0:1],
            ).reshape(chunk, layers, width)
            across = leading_divergence(values, radial_speed, chunk)
            next_ref[f, pl.ds(r, chunk)] = centre - radial_rate * across - azimuth_rate * along
        return 0

    lax.fori_loop(0, radii // chunk, body, 0)


def local(
    slabs,
    sectors,
    gas_fields,
    orbit_shift,
    particle_velocity,
    particle_mass,
    particle_stop,
    particle_cell,
    particle_dest,
):
    fields, radii, layers, sector = gas_fields.shape
    per_device = particle_dest.shape[0]
    devices = slabs * sectors
    capacity = 2 * per_device // devices
    own = radii // sectors
    rows = radii * layers
    slots = devices * capacity
    records = jnp.concatenate(
        [
            particle_velocity,
            particle_mass[None],
            particle_stop[None],
            particle_cell[None].astype(jnp.float32),
            jnp.zeros((2, per_device), jnp.float32),
        ],
        axis=0,
    )
    step = 512
    f32 = jnp.float32
    dma = pltpu.SemaphoreType.DMA
    padded, arrived_velocity, low, high = pl.pallas_call(
        functools.partial(step_kernel, slabs, sectors, step),
        out_shape=(
            jax.ShapeDtypeStruct((fields, radii + 4, layers, sector), f32),
            jax.ShapeDtypeStruct((3, slots), f32),
            jax.ShapeDtypeStruct((fields, 8, rows), f32),
            jax.ShapeDtypeStruct((fields, 8, rows), f32),
        ),
        in_specs=[in_smem] + [in_vmem] * 3,
        out_specs=(in_vmem,) * 4,
        scratch_shapes=[pltpu.VMEM((sectors, own, layers, sector), f32)] * (2 * fields)
        + [
            pltpu.VMEM((devices, 8, capacity), f32),
            pltpu.VMEM((devices, 8, capacity), f32),
            pltpu.VMEM((3 * devices * 8, capacity), f32),
            pltpu.VMEM((3 * sector, 2 * rows), jnp.bfloat16),
            pltpu.VMEM((6 * sector, rows), f32),
            pltpu.VMEM((fields, 8, rows), f32),
            pltpu.VMEM((fields, 8, rows), f32),
        ]
        + [dma((fields, sectors))] * 4
        + [dma((devices,))] * 2
        + [dma((4,))] * 2,
        compiler_params=pltpu.CompilerParams(
            vmem_limit_bytes=VMEM_LIMIT, collective_id=0, has_side_effects=True
        ),
    )(orbit_shift, gas_fields, particle_dest.reshape(1, per_device), records)
    gas_next = pl.pallas_call(
        functools.partial(transport_kernel, 4),
        out_shape=jax.ShapeDtypeStruct(gas_fields.shape, f32),
        in_specs=[in_vmem] * 3,
        out_specs=in_vmem,
        scratch_shapes=[pltpu.VMEM((fields, rows, 128), f32)],
        compiler_params=pltpu.CompilerParams(vmem_limit_bytes=VMEM_LIMIT),
    )(padded, low, high)
    return (gas_next, arrived_velocity)


def solution(mesh):
    placed = (
        P(None, "rad", None, "sec"),
        P("rad"),
        P(None, ("rad", "sec")),
        P(("rad", "sec")),
        P(("rad", "sec")),
        P(("rad", "sec")),
        P(("rad", "sec"), None),
    )
    return jax.shard_map(
        functools.partial(local, mesh.shape["rad"], mesh.shape["sec"]),
        mesh=mesh,
        in_specs=placed,
        out_specs=(P(None, "rad", None, "sec"), P(None, ("rad", "sec"))),
        check_vma=False,
    )
```

time: 218 us -> 179 us (0.82)
  other arithmetic: 24.9 us -> 0.72 us
  local copies, waits for them, and re-layouts: 18 us -> 4.75 us
  Pallas kernels: 162 us -> 173 us
  starting transfers between devices: 10.1 us -> 0 us
    pallas_call x3 -> x2, Pallas kernels: 162 us -> 173 us  [the longest x1 154 us: local(): pl.pallas_call(functools.partial(step_kernel, slabs, sectors, step), out_...]
    ppermute x4 -> x0, starting transfers between devices: 10.1 us -> none  [the longest x2 5.98 us: with_halo(): lax.ppermute(head, axis, [((i + 1) % count, i) for i in range(ends)])]
    mul x6 -> x0, other arithmetic: 9.26 us -> none  [the longest x2 7.91 us: limited_slope(): 0.5 * (jnp.sign(left_step) + jnp.sign(right_step))]
    concatenate x3 -> x0, other arithmetic: 7.24 us -> none  [the longest x2 6.85 us: with_halo(): jnp.concatenate([lax.ppermute(tail, axis, [(i, (i + 1) % count) for i in...]
    sub x3 -> x0, other arithmetic: 5.95 us -> none  [the longest x2 3.41 us: plm_divergence(): face_speed * 0.5 * (left_value + right_value)]
    ppermute x2 -> x0, local copies, waits for them, and re-layouts: 5.76 us -> none  [the longest x1 2.89 us: with_halo(): lax.ppermute(head, axis, [((i + 1) % count, i) for i in range(ends)])]
    unnamed x16 -> x7, local copies, waits for them, and re-layouts: 8.76 us -> 3.76 us
    slice x1 -> x0, local copies, waits for them, and re-layouts: 2.5 us -> none  [with_halo(): lax.slice_in_dim(cells, cells.shape[dim] - width, cells.shape[dim], axis=...]
  transfers between devices with their start and end apart: 4 -> 0, of which waited for: 0 -> 0; matrix products, arithmetic and copies ran while one was open for 11% -> 0% of each run, Pallas kernels for 0% -> 0%
where the time goes in v2:
time: 179 us
  Pallas kernels  173 us (97%)
  local copies, waits for them, and re-layouts  4.75 us (3%)
    pallas_call x1, Pallas kernels, local(): pl.pallas_call(functools.partial(step_kernel, slabs, sectors, step), out_...  154 us
    pallas_call x1, Pallas kernels, local(): pl.pallas_call(functools.partial(transport_kernel, 4), out_shape=jax.Shap...  18.3 us
    unnamed x7, local copies, waits for them, and re-layouts  3.76 us

profile of v2, /device:TPU:0, one launch (start us, length us, event | category | flops | bytes accessed | tf_op | source)
XLA Modules:
  0.0 178.7 jit_solution(12764952607896092881)
XLA Ops:
  0.6 0.7 convert_element_type.6
  1.4 1.0 concatenate.3.rec_ref
  2.3 0.0 copy-start
  2.4 1.7 copy-done
  4.1 0.0 copy-start.1
  4.1 0.7 copy-done.1
  4.8 0.0 copy-start.2
  4.8 0.7 copy-done.2
  5.5 154.3 %shard_map.86 = (f32[5,36,16,256]{3,2,1,0:T(8,128)S(1)}, f32[3,8192]{1,0:T(4,128)S(1)}, f32[5,8,512]{2,1,0:T(8,128)S(1)}, f32[5,8,512]{2,1,0:T(8,128)S(1)}) custom-call(s32[32]{0:T(128)S(1)} %copy-done.2, f32[5,32,16,256]{3,2,1,0:T(8,128)S(1)} %copy-done, s32[1,4096]{1,0:T(1,128)S(1)} %bitcast.4, f32[8,4096]{1,0:T(8,128)S(1)} %concatenate.3.rec_ref), custom_call_target="tpu_custom_call" | custom-call | tf_op jit(solution)/shard_map/pallas_call | solution.py:404
  159.7 18.3 %shard_map.87 = f32[5,32,16,256]{3,2,1,0:T(8,128)} custom-call(f32[5,36,16,256]{3,2,1,0:T(8,128)S(1)} %get-tuple-element.6.padded_ref, f32[5,8,512]{2,1,0:T(8,128)S(1)} %get-tuple-element.7.low_ref, f32[5,8,512]{2,1,0:T(8,128)S(1)} %get-tuple-element.8.high_ref), custom_call_target="tpu_custom_call" | custom-call | tf_op jit(solution)/shard_map/pallas_call | solution.py:431
  178.1 0.7 copy.10
  (1 shorter events, 0.0 us)
Async XLA Ops:
  2.3 1.7 copy-start
  4.1 0.7 copy-start.1
  4.8 0.7 copy-start.2

commit v3 on v2

--- a/solution.py
+++ b/solution.py
@@ -20,53 +20,43 @@
     return rising + jnp.minimum(jnp.maximum(left_step, right_step), 0.0)
 
 
-def face_flux(left_value, right_value, left_speed, right_speed):
+def face_weights(left_speed, right_speed):
     face_speed = 0.5 * (left_speed + right_speed)
-    return face_speed * 0.5 * (left_value + right_value) - 0.5 * (
-        jnp.abs(face_speed) + sound_speed
-    ) * (right_value - left_value)
-
-
-def leading_divergence(values, speed, extent):
+    return face_speed * 0.5, 0.5 * (jnp.abs(face_speed) + sound_speed)
+
+
+def face_flux(left_value, right_value, weights):
+    return weights[0] * (left_value + right_value) - weights[1] * (right_value - left_value)
+
+
+def leading_divergence(values, weights):
     steps = values[1:] - values[:-1]
     slopes = 0.5 * limited_slope(steps[:-1], steps[1:])
     centre = values[1:-1]
-    flux = face_flux(
-        centre[:-1] + slopes[:-1],
-        centre[1:] - slopes[1:],
-        speed[1 : extent + 2],
-        speed[2 : extent + 3],
-    )
+    flux = face_flux(centre[:-1] + slopes[:-1], centre[1:] - slopes[1:], weights)
     return flux[1:] - flux[:-1]
 
 
-def lane_divergence(values, speed, far_left, left, right, far_right, left_speed, right_speed):
+def lane_divergence(values, weights, first_step, last_step, first_flux, last_flux):
     width = values.shape[1]
     lane = lax.broadcasted_iota(jnp.int32, values.shape, 1)
     first, last = lane == 0, lane == width - 1
 
-    def after(x, end):
-        return jnp.where(last, end, pltpu.roll(x, width - 1, 1))
-
     def before(x, start):
         return jnp.where(first, start, pltpu.roll(x, 1, 1))
 
-    head, tail = values[:, 0:1], values[:, width - 1 : width]
-    following = after(values, right)
-    step = following - values
-    slopes = 0.5 * limited_slope(before(step, head - left), step)
-    end_slope = 0.5 * limited_slope(right - tail, far_right - right)
-    start_slope = 0.5 * limited_slope(left - far_left, head - left)
-    flux = face_flux(
-        values + slopes,
-        following - after(slopes, end_slope),
-        speed,
-        after(speed, right_speed),
-    )
-    start_flux = face_flux(
-        left + start_slope, head - slopes[:, 0:1], left_speed, speed[:, 0:1]
-    )
-    return flux - before(flux, start_flux)
+    step = jnp.where(last, last_step, pltpu.roll(values, width - 1, 1) - values)
+    slopes = 0.5 * limited_slope(before(step, first_step), step)
+    flux = face_flux(values + slopes, pltpu.roll(values - slopes, width - 1, 1), weights)
+    flux = jnp.where(last, last_flux, flux)
+    return flux - before(flux, first_flux)
+
+
+def boundary_flux(far_left, left, right, far_right, weights):
+    step = right - left
+    left_slope = 0.5 * limited_slope(left - far_left, step)
+    right_slope = 0.5 * limited_slope(step, far_right - right)
+    return step, face_flux(left + left_slope, right - right_slope, weights)
 
 
 def split_terms(x, terms):
@@ -127,13 +117,15 @@
     out_ref,
     low_ref,
     high_ref,
+    low_edge,
+    high_edge,
     *scratch,
 ):
     fields, radii, layers, width = gas_ref.shape
     land = scratch[:fields]
     rolled = scratch[fields : 2 * fields]
-    outbox, inbox, pack_acc, speeds, acc, low_edge, high_edge = scratch[2 * fields : 2 * fields + 7]
-    send1, recv1, send2, recv2, send3, recv3, send4, recv4 = scratch[2 * fields + 7 :]
+    outbox, inbox, pack_acc, speeds, acc = scratch[2 * fields : 2 * fields + 5]
+    send1, recv1, send2, recv2, send3, recv3, send4, recv4 = scratch[2 * fields + 5 :]
     own = radii // sectors
     rows = radii * layers
     devices = slabs * sectors
@@ -241,6 +233,7 @@
         for k, part in enumerate(split_terms(turned, 2)):
             speeds[c * width : (c + 1) * width, k * rows : (k + 1) * rows] = part
     acc[...] = jnp.zeros_like(acc)
+    step = 2 * step
     group = step // capacity
 
     def drag(i, _):
@@ -335,35 +328,49 @@
         padded_ref[:, 2 + radii : 4 + radii] = jnp.zeros((fields, 2, layers, width), jnp.float32)
 
 
-def transport_kernel(chunk, padded_ref, low_ref, high_ref, next_ref, sides):
+def transport_kernel(chunk, padded_ref, low_ref, high_ref, own_low, own_high, next_ref, sides):
     fields, radii, layers, width = next_ref.shape
     rows = chunk * layers
+
+    def cells(f):
+        west, east, head, tail = low_ref[f], high_ref[f], own_low[f], own_high[f]
+        return (west[6:7], west[7:8], head[0:1], head[1:2]), (
+            tail[6:7],
+            tail[7:8],
+            east[0:1],
+            east[1:2],
+        )
+
+    def boundary_weights(side):
+        density, momentum = cells(0)[side], cells(2)[side]
+        return face_weights(momentum[1] / density[1], momentum[2] / density[2])
+
+    pieces = []
     for f in range(fields):
-        sides[f] = jnp.concatenate([high_ref[f], low_ref[f]] * 8, axis=0).T
+        for side in range(2):
+            pieces += boundary_flux(*cells(f)[side], boundary_weights(side))
+    filler = jnp.zeros((128 - len(pieces), radii * layers), jnp.float32)
+    sides[...] = jnp.concatenate(pieces + [filler], axis=0).T
 
     def body(i, _):
         r = i * chunk
         density = padded_ref[0, pl.ds(r, chunk + 4)]
         density = jnp.where(density == 0.0, 1.0, density)
         radial_speed = padded_ref[1, pl.ds(r, chunk + 4)] / density
+        radial_weights = face_weights(radial_speed[1 : chunk + 2], radial_speed[2 : chunk + 3])
         speed = (padded_ref[2, pl.ds(r + 2, chunk)] / density[2 : 2 + chunk]).reshape(rows, width)
-        at = pl.ds(pl.multiple_of(r * layers, rows), rows)
-        end_speed = sides[2, at] / sides[0, at]
+        weights = face_weights(speed, pltpu.roll(speed, width - 1, 1))
+        side = sides[pl.ds(pl.multiple_of(r * layers, rows), rows)]
         for f in range(fields):
             values = padded_ref[f, pl.ds(r, chunk + 4)]
             centre = values[2 : 2 + chunk]
-            side = sides[f, at]
+            first_step, first_flux, last_step, last_flux = [
+                side[:, 4 * f + n : 4 * f + n + 1] for n in range(4)
+            ]
             along = lane_divergence(
-                centre.reshape(rows, width),
-                speed,
-                side[:, 14:15],
-                side[:, 15:16],
-                side[:, 0:1],
-                side[:, 1:2],
-                end_speed[:, 15:16],
-                end_speed[:, 0:1],
+                centre.reshape(rows, width), weights, first_step, last_step, first_flux, last_flux
             ).reshape(chunk, layers, width)
-            across = leading_divergence(values, radial_speed, chunk)
+            across = leading_divergence(values, radial_weights)
             next_ref[f, pl.ds(r, chunk)] = centre - radial_rate * across - azimuth_rate * along
         return 0
 
@@ -401,16 +408,15 @@
     step = 512
     f32 = jnp.float32
     dma = pltpu.SemaphoreType.DMA
-    padded, arrived_velocity, low, high = pl.pallas_call(
+    padded, arrived_velocity, *edges = pl.pallas_call(
         functools.partial(step_kernel, slabs, sectors, step),
         out_shape=(
             jax.ShapeDtypeStruct((fields, radii + 4, layers, sector), f32),
             jax.ShapeDtypeStruct((3, slots), f32),
-            jax.ShapeDtypeStruct((fields, 8, rows), f32),
-            jax.ShapeDtypeStruct((fields, 8, rows), f32),
-        ),
+        )
+        + (jax.ShapeDtypeStruct((fields, 8, rows), f32),) * 4,
         in_specs=[in_smem] + [in_vmem] * 3,
-        out_specs=(in_vmem,) * 4,
+        out_specs=(in_vmem,) * 6,
         scratch_shapes=[pltpu.VMEM((sectors, own, layers, sector), f32)] * (2 * fields)
         + [
             pltpu.VMEM((devices, 8, capacity), f32),
@@ -418,8 +424,6 @@
             pltpu.VMEM((3 * devices * 8, capacity), f32),
             pltpu.VMEM((3 * sector, 2 * rows), jnp.bfloat16),
             pltpu.VMEM((6 * sector, rows), f32),
-            pltpu.VMEM((fields, 8, rows), f32),
-            pltpu.VMEM((fields, 8, rows), f32),
         ]
         + [dma((fields, sectors))] * 4
         + [dma((devices,))] * 2
@@ -431,11 +435,11 @@
     gas_next = pl.pallas_call(
         functools.partial(transport_kernel, 4),
         out_shape=jax.ShapeDtypeStruct(gas_fields.shape, f32),
-        in_specs=[in_vmem] * 3,
+        in_specs=[in_vmem] * 5,
         out_specs=in_vmem,
-        scratch_shapes=[pltpu.VMEM((fields, rows, 128), f32)],
+        scratch_shapes=[pltpu.VMEM((rows, 128), f32)],
         compiler_params=pltpu.CompilerParams(vmem_limit_bytes=VMEM_LIMIT),
-    )(padded, low, high)
+    )(padded, *edges)
     return (gas_next, arrived_velocity)
 
 

time: 179 us -> 172 us (0.961)
  Pallas kernels: 173 us -> 165 us
    pallas_call x1, Pallas kernels: 18.3 us -> 12.8 us  [local(): pl.pallas_call(functools.partial(transport_kernel, 4), out_shape=jax.Shap...]
where the time goes in v3:
time: 172 us
  Pallas kernels  165 us (96%)
  local copies, waits for them, and re-layouts  4.75 us (3%)
    pallas_call x1, Pallas kernels, local(): pl.pallas_call(functools.partial(step_kernel, slabs, sectors, step), out_...  153 us
    pallas_call x1, Pallas kernels, local(): pl.pallas_call(functools.partial(transport_kernel, 4), out_shape=jax.Shap...  12.8 us
    unnamed x7, local copies, waits for them, and re-layouts  3.76 us

profile of v3, /device:TPU:0, one launch (start us, length us, event | category | flops | bytes accessed | tf_op | source)
XLA Modules:
  0.0 171.6 jit_solution(5774589238029405640)
XLA Ops:
  0.6 0.7 convert_element_type.6
  1.4 1.0 concatenate.3.rec_ref
  2.3 0.0 copy-start
  2.4 1.7 %copy-done = f32[5,32,16,256]{3,2,1,0:T(8,128)S(1)} copy-done((f32[5,32,16,256]{3,2,1,0:T(8,128)S(1)}, f32[5,32,16,256]{3,2,1,0:T(8,128)}, u32[]{:S(2)}) %copy-start) | copy-done | bytes 2621464
  4.1 0.0 copy-start.1
  4.1 0.7 copy-done.1
  4.8 0.0 copy-start.2
  4.8 0.7 copy-done.2
  5.5 152.6 %shard_map.86 = (f32[5,36,16,256]{3,2,1,0:T(8,128)S(1)}, f32[3,8192]{1,0:T(4,128)S(1)}, f32[5,8,512]{2,1,0:T(8,128)S(1)}, f32[5,8,512]{2,1,0:T(8,128)S(1)}, f32[...) custom-call(s32[32]{0:T(128)S(1)} %copy-done.2, f32[5,32,16,256]{3,2,1,0:T(8,128)S(1)} %copy-done, s32[1,4096]{1,0:T(1,128)S(1)} %bitcast.4, ...), custom_call_target="tpu_custom_call" | custom-call | tf_op jit(solution)/shard_map/pallas_call | solution.py:411
  158.1 12.8 %shard_map.87 = f32[5,32,16,256]{3,2,1,0:T(8,128)} custom-call(f32[5,36,16,256]{3,2,1,0:T(8,128)S(1)} %get-tuple-element.8.padded_ref, f32[5,8,512]{2,1,0:T(8,128)S(1)} %get-tuple-element.9.low_ref, f32[5,8,512]{2,1,0:T(8,128)S(1)} %get-tuple-element.10.high_ref, f32[5,8,512]{2,1,0:T(8,128)S(1)} %get-tuple-element.11.own_low, ...), custom_call_target="tpu_custom_call" | custom-call | tf_op jit(solution)/shard_map/pallas_call | solution.py:435
  170.9 0.7 copy.10
  (1 shorter events, 0.0 us)
Async XLA Ops:
  2.3 1.7 %copy-start = (f32[5,32,16,256]{3,2,1,0:T(8,128)S(1)}, f32[5,32,16,256]{3,2,1,0:T(8,128)}, u32[]{:S(2)}) copy-start(f32[5,32,16,256]{3,2,1,0:T(8,128)} %gas_ref.1) | copy-start | bytes 7864324
  4.1 0.7 copy-start.1
  4.8 0.7 copy-start.2
